TPU v7x, 256 devices: a whole 4x4x8 slice. The times are simulated.
256 devices in a mesh: tensor: 8 (over z), vocab: 32 (over x, y, core).
Axes of the slice: x: 4, y: 4, z: 8, core: 2. Of those that a mesh axis runs over, the one named last changes fastest.
Arguments:
- activated_perceptron_values: bfloat16 [2, 64, 21504], P(None, None, 'tensor'), may hold values from -6 to 6
- contraction_matrix: bfloat16 [21504, 5376], P('tensor', 'vocab'), may hold values from -0.0390625 to 0.0390625
- posterior_layer_gain: float32 [5376], P('vocab'), may hold values from -2.5 to 2.5
- skip_connection_vector: bfloat16 [2, 64, 5376], P(None, None, 'vocab'), may hold values from -6 to 6
- closing_layer_gain: float32 [5376], P('vocab'), may hold values from -2.5 to 2.5
- lexicon_matrix: bfloat16 [262144, 5376], P(('tensor', 'vocab')), may hold values from -0.25 to 0.25
- softmax_warmth: float32 [2, 64], replicated, may hold values from 0.02 to 1
- prohibited_segment_ids: int32 [2, 64, 16], replicated, may hold values from 0 to 127
- prohibited_segment_total: int32 [2, 64], replicated, may hold values from 0 to 16, as said below
- subsequent_symbol_ids: int32 [64], replicated, may hold values from 0 to 262143
Outputs:
- log_probs: float32 [2, 64, 262144], P(None, None, ('tensor', 'vocab'))
Inputs may be any that keep to these rules, and one draw needn't show every extreme that they name: `prohibited_segment_ids`: only the first prohibited_segment_total entries of a row's list count; ids may repeat. `prohibited_segment_total`: some row of each step uses all 16 slots.
All inputs are finite; a program needn't handle non-finite values.
Results may differ from a plain program's by a relative error of at most 0.00094.
Values may be sent and summed in bfloat16 or wider, within the bound.
A program may use at most 64 MiB of HBM per device.

v0:
```python
import functools

import jax
import jax.numpy as jnp
from jax import lax
from jax.experimental import pallas as pl
from jax.experimental.pallas import tpu as pltpu
from jax.sharding import PartitionSpec as P

BLOCK = 2048
NB = 16
ROWS = 128
D = 5376
COLS = 168
CHUNK = 24
PART = 176
CHIP = 336
VOC = 1024
HALF = D // 2
MESH = pl.DeviceIdType.MESH
ZLINE = (4, 3, 5, 2, 6, 1, 7, 0)
ZBOTH = (8, 9, 6, 7, 10, 11, 4, 5, 12, 13, 2, 3, 14, 15, 1)
SPREAD = (10, 11, 9, 6, 14, 2, 8, 5, 7, 13, 15, 1, 3, 4, 12)
FIRST = 0
PLANE = (10, 11, 9, 6, 14, 2, 8, 5, 7, 13, 15, 1, 3, 4, 12)
F32, BF16 = jnp.float32, jnp.bfloat16
EPS = 1e-6


def place(z, x, y, c):
    return (z, (x * 4 + y) * 2 + c)


def split16(s):
    hi = s.astype(BF16).astype(F32)
    return hi, (s - hi)


def column(value):
    n = value.shape[0]
    wide = jnp.concatenate([value, jnp.zeros((n, 256 - COLS), F32)], axis=1)
    return wide.T[:COLS]


def kernel(
    a_hbm, w_hbm, g1_hbm, skip_hbm, g2_hbm, l_hbm, warm_hbm, ids_hbm, tot_hbm, sub_hbm,
    scaled_hbm, shift_hbm,
    a_v, w_v, g1_v, skip_v, g2_v, l_v, warm_v, ids_v, tot_v, sub_v,
    skip_t, g1_t, g2_t, part, rs, sums, zb, ub, vb, nat, uacc, vacc, out_v, shift_v, la, lb, info, stat,
    in_sem, l_sem, rs_s, rs_r, zb_s, zb_r, u_s, u_r, v_s, v_r, uf_s, uf_r, vf_s, vf_r,
    la_s, la_r, lb_s, lb_r, out_sem,
):
    z = lax.axis_index("tensor")
    v = lax.axis_index("vocab")
    x, y, c = v // 8, (v // 2) % 4, v % 2
    chip = x * 4 + y
    other = 1 - c

    def copy_in(src, dst, sem):
        d = pltpu.make_async_copy(src, dst, sem)
        d.start()
        return d

    def remote(src, dst, s, r, to):
        return pltpu.make_async_remote_copy(src, dst, s, r, device_id=to, device_id_type=MESH)

    pairs = [
        (a_hbm, a_v), (w_hbm, w_v), (skip_hbm, skip_v), (g1_hbm, g1_v), (g2_hbm, g2_v),
        (warm_hbm, warm_v), (ids_hbm, ids_v), (tot_hbm, tot_v), (sub_hbm, sub_v),
    ]
    zline = [place((z + k) % 8, x, y, other) for k in range(8)]
    plane = [place(z, x ^ (k // 4), y ^ (k % 4), other) for k in range(16)]
    plane_from = [(x ^ (k // 4)) * 4 + (y ^ (k % 4)) for k in range(16)]
    zboth = [place((z + k // 2) % 8, x, y, (c + k % 2) % 2) for k in range(16)]
    sibling = plane[0]

    ins = [copy_in(s, d, in_sem.at[i]) for i, (s, d) in enumerate(pairs[:2])]
    barrier = pltpu.get_barrier_semaphore()
    for peer in [zboth[k] for k in ZBOTH] + [plane[k] for k in PLANE]:
        pl.semaphore_signal(barrier, inc=1, device_id=peer, device_id_type=MESH)

    @pl.when(c == 1)
    def _():
        for k in PLANE:
            to = place(z, x ^ (k // 4), y ^ (k % 4), 1)
            pl.semaphore_signal(barrier, inc=1, device_id=to, device_id_type=MESH)

    ins += [copy_in(s, d, in_sem.at[i + 2]) for i, (s, d) in enumerate(pairs[2:])]
    l_in = [
        copy_in(l_hbm.at[pl.ds(i * 256, 256)], l_v.at[pl.ds(i * 256, 256)], l_sem.at[i])
        for i in range(4)
    ]

    def framed(body, extra, core):
        low = jnp.concatenate([body, extra], axis=0)
        high = jnp.concatenate([extra, body], axis=0)
        return jnp.where(core == 0, low, high).astype(BF16)

    def spread(buf, core, s, r, f_s, f_r):
        own = buf.at[chip, core]
        forwards = {0: remote(own, own, f_s.at[0], f_r.at[0], sibling)}
        sends = {k: remote(own, own, s.at[k], r.at[k], plane[k]) for k in SPREAD}
        for d in [*sends.values(), forwards[0]]:
            d.start()
        return sends, forwards

    def forward(buf, core, sends, forwards, order, f_s, f_r):
        for k in order:
            sends[k].wait_recv()
            got = buf.at[plane_from[k], 1 - core]
            forwards[k] = remote(got, got, f_s.at[k], f_r.at[k], sibling)
            forwards[k].start()

    def merge(buf, pair):
        half = (x // 2) ^ pair
        forwards = v_forwards if buf is vb else u_forwards
        for k in range(pair * 8, pair * 8 + 8):
            forwards[k].wait_recv()
        total = jnp.zeros((8, ROWS), F32)
        for j in range(8):
            base = j * CHIP
            got = buf.at[half * 8 + j]
            nat[base : base + 160] = got[0, 0:160]
            e0 = got[0, 160:176].astype(F32)
            e1 = got[1, 0:16].astype(F32)
            edge = jnp.concatenate([e0[:8], e1[8:]], axis=0)
            nat[base + 160 : base + 176] = edge.astype(BF16)
            nat[base + 176 : base + 336] = got[1, 16:176]
            total = total + (e0[8:] + e1[:8])
        return total

    def product(acc, pair, tiles):
        cols = pl.ds(pl.multiple_of(((x // 2) ^ pair) * HALF, 128), HALF)
        for m in tiles:
            rows = pl.ds(m * 256, 256)
            t = jnp.dot(l_v[rows, cols], nat[...], preferred_element_type=F32)
            acc[rows] = t if pair == FIRST else acc[rows] + t

    ins[0].wait()
    ins[1].wait()
    part[:COLS] = lax.dot_general(
        w_v[...], a_v[...], (((1,), (1,)), ((), ())), preferred_element_type=F32
    )
    part[COLS:] = jnp.zeros((8 * CHUNK - COLS, ROWS), F32)
    pl.semaphore_wait(barrier, 30 + 15 * c)
    rs_sends = {}
    for k in ZLINE:
        chunk = part.at[pl.ds(pl.multiple_of((z + k) % 8 * CHUNK, 8), CHUNK)]
        rs_sends[k] = remote(chunk, rs.at[k], rs_s.at[k], rs_r.at[k], zline[k])
        rs_sends[k].start()

    for i in (2, 3, 4):
        ins[i].wait()
    skip_t[...] = column(skip_v[...].astype(F32))
    g1_t[...] = column(1.0 + jnp.broadcast_to(g1_v[...], (ROWS, COLS)))
    g2_t[...] = column(1.0 + jnp.broadcast_to(g2_v[...], (ROWS, COLS)))
    vb[chip, c] = framed(skip_t[...] * g2_t[...], jnp.zeros((8, ROWS), F32), c)
    v_sends, v_forwards = spread(vb, c, v_s, v_r, vf_s, vf_r)

    for i in (5, 6, 7, 8):
        ins[i].wait()
    block = (z * 32 + v) * VOC // BLOCK
    slot = lax.broadcasted_iota(jnp.int32, (NB, 64), 0)
    listed = []
    for s in range(2):
        hit = (ids_v[s] == block) & (slot < tot_v[s : s + 1])
        listed.append(jnp.max(jnp.where(hit, 1.0, 0.0), axis=0, keepdims=True))
    banned = jnp.concatenate(listed, axis=1)
    fed = jnp.where((sub_v[...] >> 11) == block, 1.0, 0.0)
    fed = jnp.concatenate([jnp.zeros((1, 64), F32), fed], axis=1)
    info[0:1] = jnp.maximum(banned, fed)
    warm = warm_v[...]
    info[1:2] = 1.0 / jnp.concatenate([warm[0:1], warm[1:2]], axis=1)

    total = jnp.zeros((CHUNK, ROWS), F32)
    for k in reversed(ZLINE):
        rs_sends[k].wait_recv()
        total = total + rs[k]
    sums[...] = total
    zb_sends = []
    for k in ZLINE:
        chunk = zb.at[pl.ds(pl.multiple_of(z * CHUNK, 8), CHUNK)]
        zb_sends.append(remote(sums, chunk, zb_s.at[k], zb_r.at[k], zline[k]))
        zb_sends[-1].start()
    for d in reversed(zb_sends):
        d.wait_recv()
    p = zb[:COLS]
    skip = skip_t[...]
    gained = p * g1_t[...]
    stats = [
        jnp.sum(t, axis=0, keepdims=True) for t in (p * p, skip * skip, skip * gained, gained * gained)
    ]
    hi, lo = split16(jnp.concatenate(stats, axis=0))
    ub[chip, c] = framed(gained * g2_t[...], jnp.concatenate([hi, lo], axis=0), c)
    u_sends, u_forwards = spread(ub, c, u_s, u_r, uf_s, uf_r)

    forward(vb, c, v_sends, v_forwards, SPREAD, vf_s, vf_r)
    for d in l_in:
        d.wait()
    for pair in (FIRST, 1 - FIRST):
        merge(vb, pair)
        product(vacc, pair, range(4))
    forward(ub, c, u_sends, u_forwards, SPREAD, uf_s, uf_r)
    stat[...] = merge(ub, 0)
    product(uacc, 0, range(4))
    stat[...] += merge(ub, 1)
    total = stat[:4] + stat[4:]
    r1 = lax.rsqrt(total[0:1] / D + EPS)
    square = total[1:2] + 2.0 * r1 * total[2:3] + r1 * r1 * total[3:4]
    r2 = lax.rsqrt(jnp.maximum(square, 0.0) / D + EPS)
    warmth = r2 * info[1:2]
    banned = info[0:1]
    cols = pl.ds(pl.multiple_of((1 - x // 2) * HALF, 128), HALF)
    peaks, masses = [], []
    for m in range(4):
        rows = pl.ds(m * 256, 256)
        t = jnp.dot(l_v[rows, cols], nat[...], preferred_element_type=F32)
        t = (vacc[rows] + r1 * (uacc[rows] + t)) * warmth
        vacc[rows] = t
        peaks.append(jnp.max(t, axis=0, keepdims=True))
        masses.append(jnp.sum(jnp.exp(t - peaks[m]), axis=0, keepdims=True))
    peak = functools.reduce(jnp.maximum, peaks)
    mass = sum(w * jnp.exp(q - peak) for w, q in zip(masses, peaks))
    lse = jnp.where(banned > 0.0, -1e30, peak + jnp.log(mass))

    def sent(*groups):
        for group in groups:
            for d in group:
                d.wait_send()

    def logsum(values):
        top = functools.reduce(jnp.maximum, values)
        return top + jnp.log(sum(jnp.exp(q - top) for q in values))

    la[32] = lse
    la_sends = {
        k: remote(la.at[32], la.at[2 * k + c], la_s.at[k], la_r.at[2 * k + c], place(z, x ^ (k // 4), y ^ (k % 4), 1))
        for k in PLANE + (0,)
    }
    for k in PLANE:
        la_sends[k].start()
    pl.when(c == 0)(la_sends[0].start)
    for m in range(8):
        t = vacc[pl.ds(m * 128, 128)]
        out_v[:, pl.ds(m * 128, 128)] = jnp.where(banned > 0.0, -30.0, t).T
    out_copy = copy_in(out_v, scaled_hbm, out_sem.at[0])
    sent(v_sends.values(), v_forwards.values(), rs_sends.values(), zb_sends)
    lb_sends = {
        k: remote(lb.at[8], lb.at[k // 2], lb_s.at[k], lb_r.at[k // 2], place((z + k // 2) % 8, x, y, 1 - k % 2))
        for k in ZBOTH
    }

    @pl.when(c == 1)
    def _():
        for k in (0,) + PLANE[::-1]:
            for core in (1, 0) if k else (0,):
                remote(la.at[32], la.at[2 * k + core], la_s.at[k], la_r.at[2 * k + core], sibling).wait_recv()
        lb[8] = logsum([la[j] for j in range(32) if j != 1] + [lse])
        for k in ZBOTH:
            lb_sends[k].start()
        lb[0] = lb[8]

    sent(u_sends.values(), u_forwards.values(), [la_sends[k] for k in PLANE])
    pl.when(c == 0)(la_sends[0].wait_send)
    pl.when(c == 0)(remote(lb.at[8], lb.at[0], lb_s.at[1], lb_r.at[0], sibling).wait_recv)
    for k in (1, 7, 2, 6, 3, 5, 4):
        remote(lb.at[8], lb.at[k], lb_s.at[2 * k], lb_r.at[k], sibling).wait_recv()
    lse = logsum([lb[k] for k in range(8)])
    shift_v[...] = jnp.where(banned > 0.0, 0.0, lse)
    shift_copy = copy_in(shift_v, shift_hbm, out_sem.at[1])

    @pl.when(c == 1)
    def _():
        sent(lb_sends.values())

    out_copy.wait()
    shift_copy.wait()


def local(a, w, g1, skip, g2, lexicon, warm, ids, total, sub):
    dma = pltpu.SemaphoreType.DMA
    vm = pltpu.VMEM
    scaled, shift = pl.pallas_call(
        kernel,
        name="head",
        out_shape=(
            jax.ShapeDtypeStruct((ROWS, VOC), F32),
            jax.ShapeDtypeStruct((1, ROWS), F32),
        ),
        in_specs=[pl.BlockSpec(memory_space=pl.ANY)] * 10,
        out_specs=(pl.BlockSpec(memory_space=pl.ANY),) * 2,
        scratch_shapes=[
            vm((ROWS, 2688), BF16),
            vm((COLS, 2688), BF16),
            vm((1, COLS), F32),
            vm((ROWS, COLS), BF16),
            vm((1, COLS), F32),
            vm((VOC, D), BF16),
            vm((2, 64), F32),
            vm((2, NB, 64), jnp.int32),
            vm((2, 64), jnp.int32),
            vm((1, 64), jnp.int32),
        ]
        + [vm((COLS, ROWS), F32)] * 3
        + [
            vm((8 * CHUNK, ROWS), F32),
            vm((8, CHUNK, ROWS), F32),
            vm((CHUNK, ROWS), F32),
            vm((8 * CHUNK, ROWS), F32),
            vm((16, 2, PART, ROWS), BF16),
            vm((16, 2, PART, ROWS), BF16),
            vm((HALF, ROWS), BF16),
            vm((VOC, ROWS), F32),
            vm((VOC, ROWS), F32),
            vm((ROWS, VOC), F32),
            vm((1, ROWS), F32),
            vm((33, 1, ROWS), F32),
            vm((9, 1, ROWS), F32),
            vm((8, ROWS), F32),
            vm((8, ROWS), F32),
            dma((9,)),
            dma((4,)),
        ]
        + [dma((8,))] * 4
        + [dma((16,))] * 8
        + [dma((16,)), dma((32,)), dma((16,)), dma((8,))]
        + [dma((2,))],
        compiler_params=pltpu.CompilerParams(
            collective_id=0, has_side_effects=True, vmem_limit_bytes=63 * 1024 * 1024
        ),
    )(
        a.reshape(ROWS, 2688),
        w.T,
        g1.reshape(1, COLS),
        skip.reshape(ROWS, COLS),
        g2.reshape(1, COLS),
        lexicon,
        warm,
        ids.transpose(0, 2, 1),
        total,
        sub.reshape(1, 64),
    )
    return (scaled - shift.reshape(ROWS, 1)).reshape(2, 64, VOC)


def solution(mesh):
    placed = (
        P(None, None, "tensor"),
        P("tensor", "vocab"),
        P("vocab"),
        P(None, None, "vocab"),
        P("vocab"),
        P(("tensor", "vocab"), None),
        P(),
        P(),
        P(),
        P(),
    )
    return jax.shard_map(
        local,
        mesh=mesh,
        in_specs=placed,
        out_specs=P(None, None, ("tensor", "vocab")),
        check_vma=False,
    )
```

profile of v0, /device:TPU:1, one launch (start us, length us, event | category | flops | bytes accessed | tf_op | source)
XLA Modules:
  0.0 47.6 jit_solution(13723550988041566371)
XLA Ops:
  0.0 45.6 %head.1 = (f32[128,1024]{1,0:T(8,128)}, f32[1,128]{1,0:T(1,128)}) custom-call(bf16[128,2688]{1,0:T(8,128)(2,1)} %bitcast.10, bf16[168,2688]{1,0:T(8,128)(2,1)} %bitcast.9, f32[1,168]{1,0:T(1,128)} %bitcast.13, bf16[128,168]{1,0:T(8,128)(2,1)} %bitcast.11, f32[1,168]{1,0:T(1,128)} %bitcast.14, bf16[1024,5376]{1,0:T(8,128)(2,1)} %l_hbm.1, f32[2,64]{1,0:T(2,128)} %warm_hbm.1, ...), custom_call_target="tpu_custom_call" | custom-call | tf_op jit(solution)/shard_map/head/pallas_call | solution.py:283
  45.6 1.9 %broadcast_subtract_fusion = f32[128,1024]{1,0:T(8,128)} fusion(f32[128,1024]{1,0:T(8,128)} %get-tuple-element.7, f32[128]{0:T(128)} %bitcast.16), kind=kLoop, calls=%fused_computation | loop fusion | flops 131072 | bytes 1049088 | tf_op jit(solution)/shard_map/sub | solution.py:343
where the time goes:
time: 47.7 us; the launch traced here: 47.6 us
  Pallas kernels  45.6 us (96%)
  other arithmetic  1.94 us (4%)
    pallas_call x1, Pallas kernels, local(): pl.pallas_call(kernel, name='head', out_shape=(jax.ShapeDtypeStruct((ROWS...  45.6 us
    sub x1, other arithmetic, local(): return (scaled - shift.reshape(ROWS, 1)).reshape(2, 64, VOC)  1.94 us

commit v1 on v0

--- a/solution.py
+++ b/solution.py
@@ -20,8 +20,8 @@
 MESH = pl.DeviceIdType.MESH
 ZLINE = (4, 3, 5, 2, 6, 1, 7, 0)
 ZBOTH = (8, 9, 6, 7, 10, 11, 4, 5, 12, 13, 2, 3, 14, 15, 1)
-SPREAD = (10, 11, 9, 6, 14, 2, 8, 5, 7, 13, 15, 1, 3, 4, 12)
-FIRST = 0
+SPREAD = (10, 11, 9, 14, 6, 8, 13, 15, 12, 2, 5, 7, 4, 1, 3)
+FIRST = 1
 PLANE = (10, 11, 9, 6, 14, 2, 8, 5, 7, 13, 15, 1, 3, 4, 12)
 F32, BF16 = jnp.float32, jnp.bfloat16
 EPS = 1e-6
@@ -201,16 +201,16 @@
         merge(vb, pair)
         product(vacc, pair, range(4))
     forward(ub, c, u_sends, u_forwards, SPREAD, uf_s, uf_r)
-    stat[...] = merge(ub, 0)
-    product(uacc, 0, range(4))
-    stat[...] += merge(ub, 1)
+    stat[...] = merge(ub, 1)
+    product(uacc, 1, range(4))
+    stat[...] += merge(ub, 0)
     total = stat[:4] + stat[4:]
     r1 = lax.rsqrt(total[0:1] / D + EPS)
     square = total[1:2] + 2.0 * r1 * total[2:3] + r1 * r1 * total[3:4]
     r2 = lax.rsqrt(jnp.maximum(square, 0.0) / D + EPS)
     warmth = r2 * info[1:2]
     banned = info[0:1]
-    cols = pl.ds(pl.multiple_of((1 - x // 2) * HALF, 128), HALF)
+    cols = pl.ds(pl.multiple_of(x // 2 * HALF, 128), HALF)
     peaks, masses = [], []
     for m in range(4):
         rows = pl.ds(m * 256, 256)

time: 47.7 us -> 47.5 us (level)
  no operation moved by 1% of the time
where the time goes in v1:
time: 47.5 us; the launch traced here: 47.4 us
  Pallas kernels  45.5 us (96%)
  other arithmetic  1.94 us (4%)
    pallas_call x1, Pallas kernels, local(): pl.pallas_call(kernel, name='head', out_shape=(jax.ShapeDtypeStruct((ROWS...  45.5 us
    sub x1, other arithmetic, local(): return (scaled - shift.reshape(ROWS, 1)).reshape(2, 64, VOC)  1.94 us

profile of v1, /device:TPU:1, one launch (start us, length us, event | category | flops | bytes accessed | tf_op | source)
XLA Modules:
  0.0 47.4 jit_solution(10990916170421896563)
XLA Ops:
  0.0 45.5 %head.1 = (f32[128,1024]{1,0:T(8,128)}, f32[1,128]{1,0:T(1,128)}) custom-call(bf16[128,2688]{1,0:T(8,128)(2,1)} %bitcast.10, bf16[168,2688]{1,0:T(8,128)(2,1)} %bitcast.9, f32[1,168]{1,0:T(1,128)} %bitcast.13, bf16[128,168]{1,0:T(8,128)(2,1)} %bitcast.11, f32[1,168]{1,0:T(1,128)} %bitcast.14, bf16[1024,5376]{1,0:T(8,128)(2,1)} %l_hbm.1, f32[2,64]{1,0:T(2,128)} %warm_hbm.1, ...), custom_call_target="tpu_custom_call" | custom-call | tf_op jit(solution)/shard_map/head/pallas_call | solution.py:283
  45.5 1.9 %broadcast_subtract_fusion = f32[128,1024]{1,0:T(8,128)} fusion(f32[128,1024]{1,0:T(8,128)} %get-tuple-element.7, f32[128]{0:T(128)} %bitcast.16), kind=kLoop, calls=%fused_computation | loop fusion | flops 131072 | bytes 1049088 | tf_op jit(solution)/shard_map/sub | solution.py:343
